TPU v7x, 32 devices: a whole 2x2x4 slice. The times are simulated.
32 devices in a mesh: wide: 8 (over z, y), narrow: 4 (over x, core).
Axes of the slice: x: 2, y: 2, z: 4, core: 2. Of those that a mesh axis runs over, the one named last changes fastest.
Arguments:
- file_lengths: int32 [3], replicated, may hold values from 1 to 4, as said below
- queries: bfloat16 [4096, 4096], P('wide', 'narrow'), may hold values from -6 to 6
- out_grad: bfloat16 [4096, 4096], P('wide', 'narrow'), may hold values from -6 to 6
- mem_key: bfloat16 [1024, 1024], P('wide', 'narrow'), may hold values from -6 to 6
- memory_values: bfloat16 [1024, 1024], P('wide', 'narrow'), may hold values from -6 to 6
- enc_rows: bfloat16 [1024, 4096], P('wide'), may hold values from -6 to 6
- key_down: bfloat16 [4096, 128], replicated, may hold values from -0.09375 to 0.09375
- key_up: bfloat16 [128, 1024], P(None, 'narrow'), may hold values from -0.5 to 0.5
- value_down: bfloat16 [4096, 128], replicated, may hold values from -0.09375 to 0.09375
- value_up: bfloat16 [128, 1024], P(None, 'narrow'), may hold values from -0.5 to 0.5
Outputs:
- grad_key_down: float32 [4096, 128], P('wide')
- grad_value_down: float32 [4096, 128], P('wide')
- grad_key_up: float32 [128, 1024], P(None, 'narrow')
- grad_value_up: float32 [128, 1024], P(None, 'narrow')
Inputs may be any that keep to these rules, and one draw needn't show every extreme that they name: `file_lengths`: the lengths sum to 8; the last file has 4 stretches.
All inputs are finite; a program needn't handle non-finite values.
Results may differ from a plain program's by a relative error of at most 0.0056.
Values may be sent and summed in bfloat16 or wider, within the bound.
A program may use at most 128 MiB of HBM per device.

v0:
```python
import jax
import jax.numpy as jnp
from jax import lax
from jax.sharding import PartitionSpec as P

HEAD_SIZE = 128
Q_PER_KV = 4


def passed_along(array, axis, by):
    devices = lax.axis_size(axis)
    pairs = [(i, i + by) for i in range(devices) if 0 <= i + by < devices]
    return lax.ppermute(array, axis, pairs)


def stretch_grads(query, dout, keys, values, valid):
    scale = HEAD_SIZE ** (-0.5)
    score = jnp.einsum("qgmd,kgd->gmqk", query, keys, preferred_element_type=jnp.float32) * scale
    mask = valid[None, None, None, :]
    expo = jnp.where(mask, jnp.exp(jnp.where(mask, score, 0.0)), 0.0)
    prob = expo / jnp.sum(expo, axis=-1, keepdims=True)
    prob_b = prob.astype(jnp.bfloat16)
    outp = jnp.einsum("gmqk,kgd->qgmd", prob_b, values, preferred_element_type=jnp.float32)
    delta = jnp.sum(dout.astype(jnp.float32) * outp, axis=-1)
    dprob = jnp.einsum("qgmd,kgd->gmqk", dout, values, preferred_element_type=jnp.float32)
    dscore = (prob * (dprob - jnp.transpose(delta, (1, 2, 0))[..., None])).astype(jnp.bfloat16)
    dkey = jnp.einsum("gmqk,qgmd->kgd", dscore, query, preferred_element_type=jnp.float32) * scale
    dval = jnp.einsum("gmqk,qgmd->kgd", prob_b, dout, preferred_element_type=jnp.float32)
    return (dkey, dval)


def on_device(
    file_lengths,
    queries,
    out_grad,
    mem_key,
    memory_values,
    enc_rows,
    key_down,
    key_up,
    value_down,
    value_up,
):
    wide_count = lax.axis_size("wide")
    span = min(8, wide_count // 2)
    rows = mem_key.shape[0]
    cols = mem_key.shape[1]
    local_heads = cols // HEAD_SIZE
    stretch = lax.axis_index("wide")
    starts = jnp.cumsum(file_lengths) - file_lengths
    first = jnp.max(jnp.where(starts <= stretch, starts, 0))
    position = stretch - first
    paired = jnp.stack([mem_key, memory_values])
    blocks = [paired]
    for offset in range(1, span):
        blocks.append(passed_along(paired, "wide", offset))
    window = jnp.stack(blocks)
    keys = window[:, 0].reshape(span * rows, local_heads, HEAD_SIZE)
    values = window[:, 1].reshape(span * rows, local_heads, HEAD_SIZE)
    valid = jnp.repeat(jnp.arange(span, dtype=jnp.int32) <= position, rows)
    query = queries.reshape(queries.shape[0], local_heads, Q_PER_KV, HEAD_SIZE)
    dout = out_grad.reshape(out_grad.shape[0], local_heads, Q_PER_KV, HEAD_SIZE)
    dkey, dval = stretch_grads(query, dout, keys, values, valid)
    contrib = jnp.stack([dkey.reshape(span, rows, cols), dval.reshape(span, rows, cols)], 1)
    total = contrib[0]
    for offset in range(1, span):
        total = total + passed_along(contrib[offset], "wide", -offset)
    key_grad = total[0].astype(jnp.bfloat16)
    value_grad = total[1].astype(jnp.bfloat16)
    u_key = jnp.dot(enc_rows, key_down, preferred_element_type=jnp.float32).astype(jnp.bfloat16)
    u_value = jnp.dot(enc_rows, value_down, preferred_element_type=jnp.float32).astype(jnp.bfloat16)
    part_key = jnp.dot(key_grad, key_up.T, preferred_element_type=jnp.float32)
    part_value = jnp.dot(value_grad, value_up.T, preferred_element_type=jnp.float32)
    h_key, h_value = lax.psum((part_key, part_value), "narrow")
    h_key = h_key.astype(jnp.bfloat16)
    h_value = h_value.astype(jnp.bfloat16)
    up_key = jnp.dot(u_key.T, key_grad, preferred_element_type=jnp.float32)
    up_value = jnp.dot(u_value.T, value_grad, preferred_element_type=jnp.float32)
    down_key = jnp.dot(enc_rows.T, h_key, preferred_element_type=jnp.float32)
    down_value = jnp.dot(enc_rows.T, h_value, preferred_element_type=jnp.float32)
    down_key, down_value, up_key, up_value = lax.psum(
        (down_key, down_value, up_key, up_value), "wide"
    )
    share = down_key.shape[0] // wide_count
    down_key = lax.dynamic_slice_in_dim(down_key, stretch * share, share, 0)
    down_value = lax.dynamic_slice_in_dim(down_value, stretch * share, share, 0)
    return (down_key, down_value, up_key, up_value)


def solution(mesh):
    placed = (
        P(),
        P("wide", "narrow"),
        P("wide", "narrow"),
        P("wide", "narrow"),
        P("wide", "narrow"),
        P("wide", None),
        P(),
        P(None, "narrow"),
        P(),
        P(None, "narrow"),
    )
    return jax.shard_map(
        on_device,
        mesh=mesh,
        in_specs=placed,
        out_specs=(P("wide", None), P("wide", None), P(None, "narrow"), P(None, "narrow")),
        check_vma=False,
    )
```

profile of v0, /device:TPU:0, one launch (start us, length us, event | category | flops | bytes accessed | tf_op | source)
XLA Modules:
  0.0 275.1 jit_solution(15830008956800741592)
XLA Ops:
  8.2 4.9 %collective-permute-start = (bf16[2,128,256]{2,1,0:T(8,128)(2,1)S(1)}, bf16[2,128,256]{2,1,0:T(8,128)(2,1)S(1)}, u32[]{:S(2)}, u32[]{:S(2)}) collective-permute-start(bf16[2,128,256]{2,1,0:T(8,128)(2,1)S(1)} %get-tuple-element.32), channel_id=1, source_target_pairs={{0,4},{4,8},{8,12},{12,16},{16,20},{20,24},{24,28},{1,5},{5,9},{9,... | collective-permute-start | bytes 393224 | tf_op jit(solution)/shard_map/ppermute | solution.py:13
  13.1 4.1 %collective-permute-start.1 = (bf16[2,128,256]{2,1,0:T(8,128)(2,1)S(1)}, bf16[2,128,256]{2,1,0:T(8,128)(2,1)}, u32[]{:S(2)}, u32[]{:S(2)}) collective-permute-start(bf16[2,128,256]{2,1,0:T(8,128)(2,1)S(1)} %get-tuple-element.32), channel_id=1, source_target_pairs={{0,8},{4,12},{8,16},{12,20},{16,24},{20,28},{1,9},{5,13},{9,17},{1... | collective-permute-start | bytes 393224 | tf_op jit(solution)/shard_map/ppermute | solution.py:13
  17.2 4.4 %collective-permute-start.2 = (bf16[2,128,256]{2,1,0:T(8,128)(2,1)S(1)}, bf16[2,128,256]{2,1,0:T(8,128)(2,1)}, u32[]{:S(2)}, u32[]{:S(2)}) collective-permute-start(bf16[2,128,256]{2,1,0:T(8,128)(2,1)S(1)} %get-tuple-element.32), channel_id=1, source_target_pairs={{0,12},{4,16},{8,20},{12,24},{16,28},{1,13},{5,17},{9,21},{13,25},... | collective-permute-start | bytes 393224 | tf_op jit(solution)/shard_map/ppermute | solution.py:13
  22.5 1.3 fusion.40
  24.4 1.8 reshape.47
  26.2 1.5 copy.49
  29.6 1.7 reshape_squeeze.6
  33.2 3.3 %bitcast_reduce_fusion = (f32[2,4,512]{2,1,0:T(4,128)S(1)}, f32[2,512,512,4]{2,1,3,0:T(8,128)S(1)}) fusion(pred[512]{0:T(512)(128)(4,1)S(1)} %broadcast_bitcast_fusion, bf16[512,2,4,128]{3,2,1,0:T(4,128)(2,1)S(1)} %reshape.47, bf16[512,2,128,1]{2,1,0,3:T(2,128)(2,1)} %bitcast.110), kind=kOutput, calls=%fused_computation.4 | convolution fusion | flops 545255424 | bytes 9716224 | tf_op jit(solution)/shard_map/qgmd,kgd->gmqk/dot_general | solution.py:18
  36.5 2.1 bitcast_divide_fusion
  38.6 2.6 fusion.12
  45.1 6.6 %fusion.21 = f32[512,2,128]{2,0,1:T(8,128)} fusion(f32[2,4,512,512]{2,3,1,0:T(8,128)} %copy-done.1, f32[2,4,512]{2,1,0:T(4,128)S(1)} %copy.55, bf16[512,2,128,1]{0,2,3,1:T(8,128)(2,1)S(1)} %copy.68, bf16[512,2,4,128]{0,3,2,1:T(8,128)(2,1)S(1)} %bitcast.107, bf16[512,2,4,128]{3,2,1,0:T(4,128)(2,1)S(1)} %reshape.47), kind=kOutput, calls=%fused_computation.20 | convolution fusion | flops 1080164352 | bytes 11288576 | tf_op jit(solution)/shard_map/gmqk,qgmd->kgd/dot_general | solution.py:27
  51.7 1.4 copy.57
  53.7 1.4 copy.59
  55.7 1.4 collective-permute-start.3
  57.1 1.3 collective-permute-start.4
  58.4 1.3 collective-permute-start.5
  59.7 5.2 %collective-permute-done.3 = f32[2,128,256]{2,1,0:T(8,128)S(1)} collective-permute-done((f32[2,128,256]{2,1,0:T(8,128)S(1)}, f32[2,128,256]{2,1,0:T(8,128)S(1)}, u32[]{:S(2)}, u32[]{:S(2)}) %collective-permute-start.3) | collective-permute-done | bytes 262176 | tf_op jit(solution)/shard_map/ppermute | solution.py:13
  64.9 7.9 %collective-permute-done.4 = f32[2,128,256]{2,1,0:T(8,128)S(1)} collective-permute-done((f32[2,128,256]{2,1,0:T(8,128)S(1)}, f32[2,128,256]{2,1,0:T(8,128)S(1)}, u32[]{:S(2)}, u32[]{:S(2)}) %collective-permute-start.4) | collective-permute-done | bytes 262176 | tf_op jit(solution)/shard_map/ppermute | solution.py:13
  74.0 11.6 %all-reduce.6 = (bf16[128,128]{1,0:T(8,128)(2,1)S(1)}, bf16[128,128]{1,0:T(8,128)(2,1)S(1)}) all-reduce(f32[128,128]{1,0:T(8,128)S(1)} %fusion.36, f32[128,128]{1,0:T(8,128)S(1)} %fusion.37), channel_id=1, replica_groups=mesh['wide'=8,'narrow'=4] {'narrow'}, use_global_device_ids=true, to_apply=%region_4.5 | all-reduce | flops 32768 | bytes 196608 | tf_op jit(solution)/shard_map/psum | solution.py:74
  85.6 1.8 convolution_bitcast_fusion
  87.4 1.8 convolution_bitcast_fusion.1
  91.8 170.6 %all-reduce.5.cloned.1.call-done = (f32[4096,128]{0,1:T(8,128)}, f32[4096,128]{0,1:T(8,128)}, f32[128,256]{1,0:T(8,128)}, f32[128,256]{1,0:T(8,128)}) async-done(((f32[4096,128]{0,1:T(8,128)}, f32[4096,128]{0,1:T(8,128)}, f32[128,256]{1,0:T(8,128)}, f32[128,256]{1,0:T(8,128)}), (f32[4096,128]{0,1:T(8,128)}, f32[4096,128]{0,1:T(8,128)}, f32[128,256]{1,0:T(8,128)}, ...) | async-done | bytes 4456464 | tf_op jit(solution)/shard_map/psum | solution.py:81
  265.1 1.6 copy.102
  266.7 1.6 copy.103
  (42 shorter events, 16.9 us)
Async XLA Ops:
  7.2 78.4 %copy-start = (bf16[128,4096]{1,0:T(8,128)(2,1)S(1)}, bf16[128,4096]{1,0:T(8,128)(2,1)}, u32[]{:S(2)}) copy-start(bf16[128,4096]{1,0:T(8,128)(2,1)} %param.15) | copy-start | bytes 3145732
  7.2 255.2 %all-reduce.5.cloned.1.call-start = ((), (), s32[]{:S(2)}) async-start(), calls=%async_computation | async-start | bytes 8912896 | tf_op jit(solution)/shard_map/psum | solution.py:81
  8.2 19.6 %collective-permute-start = (bf16[2,128,256]{2,1,0:T(8,128)(2,1)S(1)}, bf16[2,128,256]{2,1,0:T(8,128)(2,1)S(1)}, u32[]{:S(2)}, u32[]{:S(2)}) collective-permute-start(bf16[2,128,256]{2,1,0:T(8,128)(2,1)S(1)} %get-tuple-element.32), channel_id=1, source_target_pairs={{0,4},{4,8},{8,12},{12,16},{16,20},{20,24},{24,28},{1,5},{5,9},{9,... | collective-permute-start | bytes 393224 | tf_op jit(solution)/shard_map/ppermute | solution.py:13
  13.1 14.7 %collective-permute-start.1 = (bf16[2,128,256]{2,1,0:T(8,128)(2,1)S(1)}, bf16[2,128,256]{2,1,0:T(8,128)(2,1)}, u32[]{:S(2)}, u32[]{:S(2)}) collective-permute-start(bf16[2,128,256]{2,1,0:T(8,128)(2,1)S(1)} %get-tuple-element.32), channel_id=1, source_target_pairs={{0,8},{4,12},{8,16},{12,20},{16,24},{20,28},{1,9},{5,13},{9,17},{1... | collective-permute-start | bytes 393224 | tf_op jit(solution)/shard_map/ppermute | solution.py:13
  17.2 10.6 %collective-permute-start.2 = (bf16[2,128,256]{2,1,0:T(8,128)(2,1)S(1)}, bf16[2,128,256]{2,1,0:T(8,128)(2,1)}, u32[]{:S(2)}, u32[]{:S(2)}) collective-permute-start(bf16[2,128,256]{2,1,0:T(8,128)(2,1)S(1)} %get-tuple-element.32), channel_id=1, source_target_pairs={{0,12},{4,16},{8,20},{12,24},{16,28},{1,13},{5,17},{9,21},{13,25},... | collective-permute-start | bytes 393224 | tf_op jit(solution)/shard_map/ppermute | solution.py:13
  38.6 3.4 %copy-start.1 = (f32[2,4,512,512]{2,3,1,0:T(8,128)}, f32[2,4,512,512]{2,3,1,0:T(8,128)S(1)}, u32[]{:S(2)}) copy-start(f32[2,4,512,512]{2,3,1,0:T(8,128)S(1)} %bitcast_divide_fusion) | copy-start | bytes 25165828
  45.1 28.6 %copy-start.4 = (bf16[128,256]{1,0:T(8,128)(2,1)S(1)}, bf16[128,256]{1,0:T(8,128)(2,1)}, u32[]{:S(2)}) copy-start(bf16[128,256]{1,0:T(8,128)(2,1)} %param.17) | copy-start | bytes 196612
  45.1 28.8 %copy-start.5 = (bf16[128,256]{1,0:T(8,128)(2,1)S(1)}, bf16[128,256]{1,0:T(8,128)(2,1)}, u32[]{:S(2)}) copy-start(bf16[128,256]{1,0:T(8,128)(2,1)} %param.19) | copy-start | bytes 196612
  55.6 33.6 %copy-start.2 = (bf16[4096,128]{1,0:T(8,128)(2,1)S(1)}, bf16[4096,128]{1,0:T(8,128)(2,1)}, u32[]{:S(2)}) copy-start(bf16[4096,128]{1,0:T(8,128)(2,1)} %param.16) | copy-start | bytes 3145732
  55.7 9.2 %collective-permute-start.3 = (f32[2,128,256]{2,1,0:T(8,128)S(1)}, f32[2,128,256]{2,1,0:T(8,128)S(1)}, u32[]{:S(2)}, u32[]{:S(2)}) collective-permute-start(f32[2,128,256]{2,1,0:T(8,128)S(1)} %get-tuple-element.26), channel_id=1, source_target_pairs={{4,0},{8,4},{12,8},{16,12},{20,16},{24,20},{28,24},{5,1},{9,5},{13... | collective-permute-start | bytes 786440 | tf_op jit(solution)/shard_map/ppermute | solution.py:13
  57.1 15.7 %collective-permute-start.4 = (f32[2,128,256]{2,1,0:T(8,128)S(1)}, f32[2,128,256]{2,1,0:T(8,128)S(1)}, u32[]{:S(2)}, u32[]{:S(2)}) collective-permute-start(f32[2,128,256]{2,1,0:T(8,128)S(1)} %get-tuple-element.28), channel_id=1, source_target_pairs={{8,0},{12,4},{16,8},{20,12},{24,16},{28,20},{9,1},{13,5},{17,9},{2... | collective-permute-start | bytes 786440 | tf_op jit(solution)/shard_map/ppermute | solution.py:13
  58.4 15.2 %collective-permute-start.5 = (f32[2,128,256]{2,1,0:T(8,128)S(1)}, f32[2,128,256]{2,1,0:T(8,128)S(1)}, u32[]{:S(2)}, u32[]{:S(2)}) collective-permute-start(f32[2,128,256]{2,1,0:T(8,128)S(1)} %get-tuple-element.27), channel_id=1, source_target_pairs={{12,0},{16,4},{20,8},{24,12},{28,16},{13,1},{17,5},{21,9},{25,13},... | collective-permute-start | bytes 786440 | tf_op jit(solution)/shard_map/ppermute | solution.py:13
  73.7 16.8 %copy-start.3 = (bf16[4096,128]{1,0:T(8,128)(2,1)S(1)}, bf16[4096,128]{1,0:T(8,128)(2,1)}, u32[]{:S(2)}) copy-start(bf16[4096,128]{1,0:T(8,128)(2,1)} %param.18) | copy-start | bytes 3145732
Sparse Core Ops, SparseCore 0:
  91.9 170.4 all-reduce.4
where the time goes:
time: 276 us; the launch traced here: 275 us
  waiting for transfers between devices  185 us (67%)
  local copies, waits for them, and re-layouts  20.5 us (7%)
  matrix products  19.7 us (7%)
  starting transfers between devices  17.5 us (6%)
  between operations  14.9 us (5%)
  blocking collectives  11.6 us (4%)
  other arithmetic  6.31 us (2%)
    psum x1, waiting for transfers between devices, on_device(): lax.psum((down_key, down_value, up_key, up_value), 'wide')  171 us
    ppermute x6, starting transfers between devices, passed_along(): return lax.ppermute(array, axis, pairs)  17.5 us
    ppermute x6, waiting for transfers between devices, passed_along(): return lax.ppermute(array, axis, pairs)  13.9 us
    psum x1, blocking collectives, on_device(): h_key, h_value = lax.psum((part_key, part_value), 'narrow')  11.6 us
    unnamed x19, local copies, waits for them, and re-layouts  8.21 us
    dot_general x1, matrix products, stretch_grads(): jnp.einsum('gmqk,qgmd->kgd', dscore, query, preferred_element_type=jnp.fl...  6.64 us
  transfers between devices with their start and end apart: 7, of which 4 were waited for; matrix products, arithmetic and copies ran while one was open for 2% of the time, Pallas kernels for 0%

commit v1 on v0

v1 whole, which is shorter than its diff:
```python
import functools
import math

import jax
import jax.numpy as jnp
from jax import lax
from jax.experimental import pallas as pl
from jax.experimental.pallas import tpu as pltpu
from jax.sharding import PartitionSpec as P

HEAD_SIZE = 128
Q_PER_KV = 4
F32 = jnp.float32
BF16 = jnp.bfloat16
MESH = pl.DeviceIdType.MESH


def position_of(file_lengths, stretch):
    files = file_lengths.shape[0]
    start = jnp.int32(0)
    first = jnp.int32(0)
    for f in range(files):
        first = jnp.where(start <= stretch, start, first)
        start = start + file_lengths[f]
    return stretch - first


def passed_along(array, axis, by):
    devices = lax.axis_size(axis)
    pairs = [(i, i + by) for i in range(devices) if 0 <= i + by < devices]
    return lax.ppermute(array, axis, pairs)


def stretch_grads(query, dout, keys, values, valid):
    scale = HEAD_SIZE ** (-0.5)
    score = jnp.einsum("qgmd,kgd->gmqk", query, keys, preferred_element_type=F32) * scale
    mask = valid[None, None, None, :]
    expo = jnp.where(mask, jnp.exp(jnp.where(mask, score, 0.0)), 0.0)
    prob = expo / jnp.sum(expo, axis=-1, keepdims=True)
    prob_b = prob.astype(BF16)
    outp = jnp.einsum("gmqk,kgd->qgmd", prob_b, values, preferred_element_type=F32)
    delta = jnp.sum(dout.astype(F32) * outp, axis=-1)
    dprob = jnp.einsum("qgmd,kgd->gmqk", dout, values, preferred_element_type=F32)
    dscore = (prob * (dprob - jnp.transpose(delta, (1, 2, 0))[..., None])).astype(BF16)
    dkey = jnp.einsum("gmqk,qgmd->kgd", dscore, query, preferred_element_type=F32) * scale
    dval = jnp.einsum("gmqk,qgmd->kgd", prob_b, dout, preferred_element_type=F32)
    return (dkey, dval)


def by_collectives(file_lengths, queries, out_grad, mem_key, memory_values, enc_rows, key_down, key_up, value_down, value_up):
    wide_count = lax.axis_size("wide")
    span = min(8, wide_count // 2)
    rows, cols = mem_key.shape
    local_heads = cols // HEAD_SIZE
    stretch = lax.axis_index("wide")
    position = position_of(file_lengths, stretch)
    paired = jnp.stack([mem_key, memory_values])
    blocks = [paired]
    for offset in range(1, span):
        blocks.append(passed_along(paired, "wide", offset))
    window = jnp.stack(blocks)
    keys = window[:, 0].reshape(span * rows, local_heads, HEAD_SIZE)
    values = window[:, 1].reshape(span * rows, local_heads, HEAD_SIZE)
    valid = jnp.repeat(jnp.arange(span, dtype=jnp.int32) <= position, rows)
    query = queries.reshape(queries.shape[0], local_heads, Q_PER_KV, HEAD_SIZE)
    dout = out_grad.reshape(out_grad.shape[0], local_heads, Q_PER_KV, HEAD_SIZE)
    dkey, dval = stretch_grads(query, dout, keys, values, valid)
    contrib = jnp.stack([dkey.reshape(span, rows, cols), dval.reshape(span, rows, cols)], 1)
    total = contrib[0]
    for offset in range(1, span):
        total = total + passed_along(contrib[offset], "wide", -offset)
    key_grad = total[0].astype(BF16)
    value_grad = total[1].astype(BF16)
    u_key = jnp.dot(enc_rows, key_down, preferred_element_type=F32).astype(BF16)
    u_value = jnp.dot(enc_rows, value_down, preferred_element_type=F32).astype(BF16)
    part_key = jnp.dot(key_grad, key_up.T, preferred_element_type=F32)
    part_value = jnp.dot(value_grad, value_up.T, preferred_element_type=F32)
    h_key, h_value = lax.psum((part_key, part_value), "narrow")
    h_key = h_key.astype(BF16)
    h_value = h_value.astype(BF16)
    up_key = jnp.dot(u_key.T, key_grad, preferred_element_type=F32)
    up_value = jnp.dot(u_value.T, value_grad, preferred_element_type=F32)
    down_key = jnp.dot(enc_rows.T, h_key, preferred_element_type=F32)
    down_value = jnp.dot(enc_rows.T, h_value, preferred_element_type=F32)
    down_key, down_value, up_key, up_value = lax.psum((down_key, down_value, up_key, up_value), "wide")
    share = down_key.shape[0] // wide_count
    down_key = lax.dynamic_slice_in_dim(down_key, stretch * share, share, 0)
    down_value = lax.dynamic_slice_in_dim(down_value, stretch * share, share, 0)
    return (down_key, down_value, up_key, up_value)


NT = (((1,), (1,)), ((), ()))
TN = (((0,), (0,)), ((), ()))


def kernel(
    W, N, span,
    lengths, q_hbm, g_hbm, k_hbm, v_hbm, enc_hbm, kd_hbm, ku_hbm, vd_hbm, vu_hbm,
    okd, ovd, oku, ovu,
    q_v, g_v, kwin, vwin, enc_v, down_v, up_v,
    enc_slots, dk_acc, dv_acc, c_send, c_recv, u_v, kg_v,
    part32, part_send, part_recv, h_slots, rs_send, rs_recv, fin, res,
    local_sem, kv_s, kv_r, enc_s, enc_r, c_s, c_r, part_s, part_r, h_s, h_r, rs_s, rs_r, ag_s, ag_r, res_s, res_r,
):
    w = lax.axis_index("wide")
    n = lax.axis_index("narrow")
    half, kind = n // 2, n % 2
    rows, cols = k_hbm.shape
    groups = cols // HEAD_SIZE
    share = okd.shape[0]
    part_cols = share // 2
    rank = kd_hbm.shape[1]
    piece = rank // W
    scale = HEAD_SIZE ** (-0.5)

    def my_cols(owner):
        return pl.ds(pl.multiple_of(owner * share + half * part_cols, part_cols), part_cols)

    def local(i, src, dst):
        c = pltpu.make_async_copy(src, dst, local_sem.at[i])
        c.start()
        return c

    l_k = local(0, k_hbm, kwin.at[0])
    l_v = local(1, v_hbm, vwin.at[0])
    l_enc = local(2, enc_hbm, enc_v)
    l_kd = local(3, kd_hbm, down_v.at[:, pl.ds(0, rank)])
    l_vd = local(4, vd_hbm, down_v.at[:, pl.ds(rank, rank)])
    l_q = local(5, q_hbm, q_v)
    l_g = local(6, g_hbm, g_v)
    l_ku = local(7, ku_hbm, up_v.at[0])
    l_vu = local(8, vu_hbm, up_v.at[1])
    l_own = local(9, enc_hbm.at[:, my_cols(w)], enc_slots.at[0])

    barrier = pltpu.get_barrier_semaphore()
    for o in range(1, W):
        pl.semaphore_signal(barrier, inc=1, device_id=((w + o) % W, n), device_id_type=MESH)
    for o in range(1, N):
        pl.semaphore_signal(barrier, inc=1, device_id=(w, (n + o) % N), device_id_type=MESH)
    pl.semaphore_wait(barrier, W - 1 + N - 1)

    def remote(src, dst, ss, rs, to):
        return pltpu.make_async_remote_copy(
            src_ref=src, dst_ref=dst, send_sem=ss, recv_sem=rs, device_id=to, device_id_type=MESH
        )

    def kv_copy(j, t):
        src, dst = ((k_hbm, kwin), (v_hbm, vwin))[t]
        return remote(src, dst.at[j], kv_s.at[j, t], kv_r.at[j, t], ((w + j) % W, n))

    for j in range(1, span):
        @pl.when(w + j < W)
        def _():
            kv_copy(j, 0).start()
            kv_copy(j, 1).start()

        @pl.when(w < j)
        def _():
            kwin[j] = jnp.zeros((rows, cols), BF16)
            vwin[j] = jnp.zeros((rows, cols), BF16)

        @pl.when(w + j >= W)
        def _():
            for g in range(groups):
                c_recv[g, j] = jnp.zeros((2, rows, HEAD_SIZE), BF16)

    def enc_copy(o):
        to = (w + o) % W
        return remote(enc_hbm.at[:, my_cols(to)], enc_slots.at[o], enc_s.at[o], enc_r.at[o], (to, n))

    for o in range(1, W):
        enc_copy(o).start()

    l_enc.wait()
    l_kd.wait()
    l_vd.wait()
    u_v[...] = jnp.dot(enc_v[...], down_v[...], preferred_element_type=F32).astype(BF16)

    position = position_of(lengths, w)
    bias = [jnp.where(j <= position, 0.0, -1e30).astype(F32) for j in range(span)]
    l_k.wait()
    l_v.wait()
    l_q.wait()
    l_g.wait()
    for j in range(1, span):
        @pl.when(w >= j)
        def _():
            kv_copy(j, 0).wait_recv()
            kv_copy(j, 1).wait_recv()

    factor = scale * math.log2(math.e)
    chunk = 256
    n_chunks = q_v.shape[0] // chunk

    def c_copy(g, j):
        return remote(c_send.at[g, j], c_recv.at[g, j], c_s.at[g, j], c_r.at[g, j], ((w + W - j) % W, n))

    for g in range(groups):
        head_cols = slice(g * HEAD_SIZE, (g + 1) * HEAD_SIZE)
        dk_acc[g] = jnp.zeros((span * rows, HEAD_SIZE), F32)
        dv_acc[g] = jnp.zeros((span * rows, HEAD_SIZE), F32)

        def head(m, carry):
            col = pl.ds(pl.multiple_of((g * Q_PER_KV + m) * HEAD_SIZE, HEAD_SIZE), HEAD_SIZE)
            kg = kwin[:, :, head_cols].reshape(span * rows, HEAD_SIZE)
            vg = vwin[:, :, head_cols].reshape(span * rows, HEAD_SIZE)
            for c in range(n_chunks):
                qh = q_v[c * chunk:(c + 1) * chunk, col]
                dh = g_v[c * chunk:(c + 1) * chunk, col]
                s = lax.dot_general(kg, qh, NT, preferred_element_type=F32)
                dp = lax.dot_general(vg, dh, NT, preferred_element_type=F32)
                t = jnp.concatenate(
                    [s[j * rows:(j + 1) * rows] * factor + (bias[j] if j else 0.0) for j in range(span)], 0
                )
                e = jnp.exp2(t)
                r = 1.0 / jnp.sum(e, axis=0, keepdims=True)
                delta = jnp.sum(e * dp, axis=0, keepdims=True) * r
                p = e * r
                ds = (p * (dp - delta)).astype(BF16)
                dv_acc[g] += jnp.dot(p.astype(BF16), dh, preferred_element_type=F32)
                dk_acc[g] += jnp.dot(ds, qh, preferred_element_type=F32)
            return carry

        lax.fori_loop(0, Q_PER_KV, head, 0)
        for j in range(1, span):
            c_send[g, j, 0] = (dk_acc[g, j * rows:(j + 1) * rows] * scale).astype(BF16)
            c_send[g, j, 1] = dv_acc[g, j * rows:(j + 1) * rows].astype(BF16)

            @pl.when(w >= j)
            def _():
                c_copy(g, j).start()

    for g in range(groups):
        for j in range(1, span):
            @pl.when(w + j < W)
            def _():
                c_copy(g, j).wait_recv()

        key_total = dk_acc[g, :rows] * scale
        value_total = dv_acc[g, :rows]
        for j in range(1, span):
            key_total = key_total + c_recv[g, j, 0].astype(F32)
            value_total = value_total + c_recv[g, j, 1].astype(F32)
        kg_v[0, :, g * HEAD_SIZE:(g + 1) * HEAD_SIZE] = key_total.astype(BF16)
        kg_v[1, :, g * HEAD_SIZE:(g + 1) * HEAD_SIZE] = value_total.astype(BF16)

    l_ku.wait()
    l_vu.wait()
    for t in range(2):
        part = lax.dot_general(kg_v[t], up_v[t], NT, preferred_element_type=F32)
        part32[t] = part
        part_send[t] = part.astype(BF16)

    def part_copy(o):
        to = (n + o) % N
        return remote(part_send.at[to % 2], part_recv.at[o], part_s.at[o], part_r.at[o], (w, to))

    for o in range(1, N):
        part_copy(o).start()

    for t in range(2):
        up = lax.dot_general(u_v[:, t * rank:(t + 1) * rank], kg_v[t], TN, preferred_element_type=F32).astype(BF16)
        for i in range(W):
            rs_send[i, t] = up[i * piece:(i + 1) * piece]

    def rs_copy(o):
        to = (w + o) % W
        return remote(rs_send.at[to], rs_recv.at[o], rs_s.at[o], rs_r.at[o], (to, n))

    for o in range(1, W):
        rs_copy(o).start()

    total = part32[kind]
    for o in range(1, N):
        part_copy(o).wait_recv()
        total = total + part_recv[o].astype(F32)
    h_slots[0] = total.astype(BF16)

    def h_copy(o):
        return remote(h_slots.at[0], h_slots.at[o], h_s.at[o], h_r.at[o], ((w + o) % W, n))

    for o in range(1, W):
        h_copy(o).start()

    total = rs_send[w].astype(F32)
    for o in range(1, W):
        rs_copy(o).wait_recv()
        total = total + rs_recv[o].astype(F32)
    fin[w] = total.astype(BF16)

    def ag_copy(o, at):
        return remote(fin.at[w], fin.at[at], ag_s.at[o], ag_r.at[o], ((w + o) % W, n))

    for o in range(1, W):
        ag_copy(o, w).start()

    l_own.wait()
    for o in range(1, W):
        enc_copy(o).wait_recv()
        h_copy(o).wait_recv()
    down = lax.dot_general(
        enc_slots[...].reshape(W * rows, part_cols), h_slots[...].reshape(W * rows, rank), TN,
        preferred_element_type=F32,
    )
    res[n] = down.astype(BF16)

    def res_copy(o, at):
        return remote(res.at[n], res.at[at], res_s.at[o], res_r.at[o], (w, (n + o) % N))

    for o in range(1, N):
        res_copy(o, n).start()

    for o in range(1, W):
        ag_copy(o, (w + W - o) % W).wait_recv()
    for i in range(W):
        oku[i * piece:(i + 1) * piece, :] = fin[i, 0].astype(F32)
        ovu[i * piece:(i + 1) * piece, :] = fin[i, 1].astype(F32)
    for o in range(1, N):
        res_copy(o, (n + N - o) % N).wait_recv()
    for i in range(N):
        (okd, ovd)[i % 2][(i // 2) * part_cols:(i // 2 + 1) * part_cols, :] = res[i].astype(F32)

    for j in range(1, span):
        @pl.when(w + j < W)
        def _():
            kv_copy(j, 0).wait_send()
            kv_copy(j, 1).wait_send()

        @pl.when(w >= j)
        def _():
            for g in range(groups):
                c_copy(g, j).wait_send()
    for o in range(1, W):
        enc_copy(o).wait_send()
        rs_copy(o).wait_send()
        h_copy(o).wait_send()
        ag_copy(o, w).wait_send()
    for o in range(1, N):
        part_copy(o).wait_send()
        res_copy(o, n).wait_send()


def by_kernel(file_lengths, queries, out_grad, mem_key, memory_values, enc_rows, key_down, key_up, value_down, value_up):
    W, N = lax.axis_size("wide"), lax.axis_size("narrow")
    span = min(8, W // 2)
    rows, cols = mem_key.shape
    groups = cols // HEAD_SIZE
    width, rank = key_down.shape
    share = width // W
    half = share // 2
    piece = rank // W
    dma = pltpu.SemaphoreType.DMA
    any_spec = pl.BlockSpec(memory_space=pl.ANY)
    vmem_spec = pl.BlockSpec(memory_space=pltpu.VMEM)
    return pl.pallas_call(
        functools.partial(kernel, W, N, span),
        out_shape=(
            jax.ShapeDtypeStruct((share, rank), F32),
            jax.ShapeDtypeStruct((share, rank), F32),
            jax.ShapeDtypeStruct((rank, cols), F32),
            jax.ShapeDtypeStruct((rank, cols), F32),
        ),
        in_specs=[pl.BlockSpec(memory_space=pltpu.SMEM)] + [any_spec] * 9,
        out_specs=(vmem_spec,) * 4,
        scratch_shapes=[
            pltpu.VMEM(queries.shape, BF16),
            pltpu.VMEM(out_grad.shape, BF16),
            pltpu.VMEM((span, rows, cols), BF16),
            pltpu.VMEM((span, rows, cols), BF16),
            pltpu.VMEM((rows, width), BF16),
            pltpu.VMEM((width, 2 * rank), BF16),
            pltpu.VMEM((2, rank, cols), BF16),
            pltpu.VMEM((W, rows, half), BF16),
            pltpu.VMEM((groups, span * rows, HEAD_SIZE), F32),
            pltpu.VMEM((groups, span * rows, HEAD_SIZE), F32),
            pltpu.VMEM((groups, span, 2, rows, HEAD_SIZE), BF16),
            pltpu.VMEM((groups, span, 2, rows, HEAD_SIZE), BF16),
            pltpu.VMEM((rows, 2 * rank), BF16),
            pltpu.VMEM((2, rows, cols), BF16),
            pltpu.VMEM((2, rows, rank), F32),
            pltpu.VMEM((2, rows, rank), BF16),
            pltpu.VMEM((N, rows, rank), BF16),
            pltpu.VMEM((W, rows, rank), BF16),
            pltpu.VMEM((W, 2, piece, cols), BF16),
            pltpu.VMEM((W, 2, piece, cols), BF16),
            pltpu.VMEM((W, 2, piece, cols), BF16),
            pltpu.VMEM((N, half, rank), BF16),
            dma((10,)),
            dma((span, 2)), dma((span, 2)),
            dma((W,)), dma((W,)),
            dma((groups, span)), dma((groups, span)),
            dma((N,)), dma((N,)),
            dma((W,)), dma((W,)),
            dma((W,)), dma((W,)),
            dma((W,)), dma((W,)),
            dma((N,)), dma((N,)),
        ],
        compiler_params=pltpu.CompilerParams(
            collective_id=0, has_side_effects=True, vmem_limit_bytes=48 * 2**20
        ),
    )(file_lengths, queries, out_grad, mem_key, memory_values, enc_rows, key_down, key_up, value_down, value_up)


def solution(mesh):
    placed = (
        P(),
        P("wide", "narrow"),
        P("wide", "narrow"),
        P("wide", "narrow"),
        P("wide", "narrow"),
        P("wide", None),
        P(),
        P(None, "narrow"),
        P(),
        P(None, "narrow"),
    )

    def on_device(*args):
        W, N = lax.axis_size("wide"), lax.axis_size("narrow")
        width, rank = args[6].shape
        fits = N == 4 and width % (W * 256) == 0 and rank % (W * 16) == 0 and args[1].shape[0] % 256 == 0
        return (by_kernel if fits else by_collectives)(*args)

    return jax.shard_map(
        on_device,
        mesh=mesh,
        in_specs=placed,
        out_specs=(P("wide", None), P("wide", None), P(None, "narrow"), P(None, "narrow")),
        check_vma=False,
    )
```

time: 276 us -> 66.6 us (0.24)
  waiting for transfers between devices: 185 us -> 0 us
  Pallas kernels: 0 us -> 53.8 us
  matrix products: 19.7 us -> 0 us
  starting transfers between devices: 17.5 us -> 0 us
  between operations: 14.9 us -> 0.66 us
  blocking collectives: 11.6 us -> 0 us
  local copies, waits for them, and re-layouts: 20.5 us -> 11.6 us
  other arithmetic: 6.31 us -> 0 us
    psum x1 -> x0, waiting for transfers between devices: 171 us -> none  [on_device(): lax.psum((down_key, down_value, up_key, up_value), 'wide')]
    pallas_call x0 -> x1, Pallas kernels: none -> 53.8 us  [by_kernel(): pl.pallas_call(functools.partial(kernel, W, N, span), out_shape=(jax.Shap...]
    dot_general x10 -> x0, matrix products: 19.7 us -> none  [the longest x1 6.64 us: stretch_grads(): jnp.einsum('gmqk,qgmd->kgd', dscore, query, preferred_element_type=jnp.fl...]
    ppermute x6 -> x0, starting transfers between devices: 17.5 us -> none  [passed_along(): return lax.ppermute(array, axis, pairs)]
    ppermute x6 -> x0, waiting for transfers between devices: 13.9 us -> none  [passed_along(): return lax.ppermute(array, axis, pairs)]
    psum x1 -> x0, blocking collectives: 11.6 us -> none  [on_device(): h_key, h_value = lax.psum((part_key, part_value), 'narrow')]
    another operation x6 -> x0, local copies, waits for them, and re-layouts: 4.47 us -> none  [the longest x2 1.88 us: on_device(): values = window[:, 1].reshape(span * rows, local_heads, HEAD_SIZE)]
    unnamed x19 -> x22, local copies, waits for them, and re-layouts: 8.21 us -> 11.6 us
  transfers between devices with their start and end apart: 7 -> 0, of which waited for: 4 -> 0; matrix products, arithmetic and copies ran while one was open for 2% -> 0% of each run, Pallas kernels for 0% -> 0%
where the time goes in v1:
time: 66.6 us; the launch traced here: 66.1 us
  Pallas kernels  53.8 us (81%)
  local copies, waits for them, and re-layouts  11.6 us (17%)
    pallas_call x1, Pallas kernels, by_kernel(): pl.pallas_call(functools.partial(kernel, W, N, span), out_shape=(jax.Shap...  53.8 us
    unnamed x22, local copies, waits for them, and re-layouts  11.6 us

profile of v1, /device:TPU:0, one launch (start us, length us, event | category | flops | bytes accessed | tf_op | source)
XLA Modules:
  0.0 66.1 jit_solution(3393655192190401324)
XLA Ops:
  0.6 0.0 copy-start
  0.6 1.2 %copy-done = bf16[512,1024]{1,0:T(8,128)(2,1)S(1)} copy-done((bf16[512,1024]{1,0:T(8,128)(2,1)S(1)}, bf16[512,1024]{1,0:T(8,128)(2,1)}, u32[]{:S(2)}) %copy-start) | copy-done | bytes 1048600
  1.9 0.0 copy-start.1
  1.9 1.2 %copy-done.1 = bf16[512,1024]{1,0:T(8,128)(2,1)S(1)} copy-done((bf16[512,1024]{1,0:T(8,128)(2,1)S(1)}, bf16[512,1024]{1,0:T(8,128)(2,1)}, u32[]{:S(2)}) %copy-start.1) | copy-done | bytes 1048600
  3.1 0.0 copy-start.2
  3.1 1.2 %copy-done.2 = bf16[128,4096]{1,0:T(8,128)(2,1)S(1)} copy-done((bf16[128,4096]{1,0:T(8,128)(2,1)S(1)}, bf16[128,4096]{1,0:T(8,128)(2,1)}, u32[]{:S(2)}) %copy-start.2) | copy-done | bytes 1048600
  4.3 0.0 copy-start.3
  4.3 1.2 %copy-done.3 = bf16[4096,128]{1,0:T(8,128)(2,1)S(1)} copy-done((bf16[4096,128]{1,0:T(8,128)(2,1)S(1)}, bf16[4096,128]{1,0:T(8,128)(2,1)}, u32[]{:S(2)}) %copy-start.3) | copy-done | bytes 1048600
  5.5 0.0 copy-start.4
  5.5 0.8 %copy-done.4 = bf16[128,256]{1,0:T(8,128)(2,1)S(1)} copy-done((bf16[128,256]{1,0:T(8,128)(2,1)S(1)}, bf16[128,256]{1,0:T(8,128)(2,1)}, u32[]{:S(2)}) %copy-start.4) | copy-done | bytes 65560
  6.4 0.0 copy-start.5
  6.4 0.8 %copy-done.5 = bf16[128,256]{1,0:T(8,128)(2,1)S(1)} copy-done((bf16[128,256]{1,0:T(8,128)(2,1)S(1)}, bf16[128,256]{1,0:T(8,128)(2,1)}, u32[]{:S(2)}) %copy-start.5) | copy-done | bytes 65560
  7.2 0.0 copy-start.6
  7.2 0.8 %copy-done.6 = bf16[128,256]{1,0:T(8,128)(2,1)S(1)} copy-done((bf16[128,256]{1,0:T(8,128)(2,1)S(1)}, bf16[128,256]{1,0:T(8,128)(2,1)}, u32[]{:S(2)}) %copy-start.6) | copy-done | bytes 65560
  8.1 0.0 copy-start.7
  8.1 0.8 %copy-done.7 = bf16[128,256]{1,0:T(8,128)(2,1)S(1)} copy-done((bf16[128,256]{1,0:T(8,128)(2,1)S(1)}, bf16[128,256]{1,0:T(8,128)(2,1)}, u32[]{:S(2)}) %copy-start.7) | copy-done | bytes 65560
  8.9 0.0 copy-start.8
  8.9 0.7 copy-done.8
  9.6 53.8 %shard_map.129 = (f32[512,128]{1,0:T(8,128)S(1)}, f32[512,128]{1,0:T(8,128)S(1)}, f32[128,256]{1,0:T(8,128)S(1)}, f32[128,256]{1,0:T(8,128)S(1)}) custom-call(s32[3]{0:T(128)S(1)} %copy-done.8, bf16[512,1024]{1,0:T(8,128)(2,1)S(1)} %copy-done, bf16[512,1024]{1,0:T(8,128)(2,1)S(1)} %copy-done.1, bf16[128,256]{1,0:T(8,128)(2,1)S(1)} %copy-done.4, ...), custom_call_target="tpu_custom_call" | custom-call | tf_op jit(solution)/shard_map/pallas_call | solution.py:355
  63.4 0.7 %copy.18 = f32[512,128]{1,0:T(8,128)} copy(f32[512,128]{1,0:T(8,128)S(1)} %get-tuple-element.8) | data formatting | bytes 524288
  64.1 0.7 %copy.19 = f32[512,128]{1,0:T(8,128)} copy(f32[512,128]{1,0:T(8,128)S(1)} %get-tuple-element.9) | data formatting | bytes 524288
  64.8 0.7 copy.20
  65.4 0.7 copy.21
Async XLA Ops:
  0.6 1.2 %copy-start = (bf16[512,1024]{1,0:T(8,128)(2,1)S(1)}, bf16[512,1024]{1,0:T(8,128)(2,1)}, u32[]{:S(2)}) copy-start(bf16[512,1024]{1,0:T(8,128)(2,1)} %q_hbm.1) | copy-start | bytes 3145732
  1.9 1.2 %copy-start.1 = (bf16[512,1024]{1,0:T(8,128)(2,1)S(1)}, bf16[512,1024]{1,0:T(8,128)(2,1)}, u32[]{:S(2)}) copy-start(bf16[512,1024]{1,0:T(8,128)(2,1)} %g_hbm.1) | copy-start | bytes 3145732
  3.1 1.2 %copy-start.2 = (bf16[128,4096]{1,0:T(8,128)(2,1)S(1)}, bf16[128,4096]{1,0:T(8,128)(2,1)}, u32[]{:S(2)}) copy-start(bf16[128,4096]{1,0:T(8,128)(2,1)} %enc_hbm.1) | copy-start | bytes 3145732
  4.3 1.2 %copy-start.3 = (bf16[4096,128]{1,0:T(8,128)(2,1)S(1)}, bf16[4096,128]{1,0:T(8,128)(2,1)}, u32[]{:S(2)}) copy-start(bf16[4096,128]{1,0:T(8,128)(2,1)} %kd_hbm.1) | copy-start | bytes 3145732
  5.5 0.8 %copy-start.4 = (bf16[128,256]{1,0:T(8,128)(2,1)S(1)}, bf16[128,256]{1,0:T(8,128)(2,1)}, u32[]{:S(2)}) copy-start(bf16[128,256]{1,0:T(8,128)(2,1)} %k_hbm.1) | copy-start | bytes 196612
  6.4 0.8 %copy-start.5 = (bf16[128,256]{1,0:T(8,128)(2,1)S(1)}, bf16[128,256]{1,0:T(8,128)(2,1)}, u32[]{:S(2)}) copy-start(bf16[128,256]{1,0:T(8,128)(2,1)} %v_hbm.1) | copy-start | bytes 196612
  7.2 0.8 %copy-start.6 = (bf16[128,256]{1,0:T(8,128)(2,1)S(1)}, bf16[128,256]{1,0:T(8,128)(2,1)}, u32[]{:S(2)}) copy-start(bf16[128,256]{1,0:T(8,128)(2,1)} %ku_hbm.1) | copy-start | bytes 196612
  8.1 0.8 %copy-start.7 = (bf16[128,256]{1,0:T(8,128)(2,1)S(1)}, bf16[128,256]{1,0:T(8,128)(2,1)}, u32[]{:S(2)}) copy-start(bf16[128,256]{1,0:T(8,128)(2,1)} %vu_hbm.1) | copy-start | bytes 196612
  8.9 0.7 copy-start.8

commit v2 on v1

--- a/solution.py
+++ b/solution.py
@@ -96,10 +96,10 @@
 def kernel(
     W, N, span,
     lengths, q_hbm, g_hbm, k_hbm, v_hbm, enc_hbm, kd_hbm, ku_hbm, vd_hbm, vu_hbm,
-    okd, ovd, oku, ovu,
+    res, fin,
     q_v, g_v, kwin, vwin, enc_v, down_v, up_v,
     enc_slots, dk_acc, dv_acc, c_send, c_recv, u_v, kg_v,
-    part32, part_send, part_recv, h_slots, rs_send, rs_recv, fin, res,
+    part32, part_send, part_recv, h_slots, rs_send, rs_recv,
     local_sem, kv_s, kv_r, enc_s, enc_r, c_s, c_r, part_s, part_r, h_s, h_r, rs_s, rs_r, ag_s, ag_r, res_s, res_r,
 ):
     w = lax.axis_index("wide")
@@ -107,8 +107,8 @@
     half, kind = n // 2, n % 2
     rows, cols = k_hbm.shape
     groups = cols // HEAD_SIZE
-    share = okd.shape[0]
-    part_cols = share // 2
+    part_cols = res.shape[1]
+    share = 2 * part_cols
     rank = kd_hbm.shape[1]
     piece = rank // W
     scale = HEAD_SIZE ** (-0.5)
@@ -187,7 +187,6 @@
         def _():
             kv_copy(j, 0).wait_recv()
             kv_copy(j, 1).wait_recv()
-
     factor = scale * math.log2(math.e)
     chunk = 256
     n_chunks = q_v.shape[0] // chunk
@@ -312,13 +311,8 @@
 
     for o in range(1, W):
         ag_copy(o, (w + W - o) % W).wait_recv()
-    for i in range(W):
-        oku[i * piece:(i + 1) * piece, :] = fin[i, 0].astype(F32)
-        ovu[i * piece:(i + 1) * piece, :] = fin[i, 1].astype(F32)
     for o in range(1, N):
         res_copy(o, (n + N - o) % N).wait_recv()
-    for i in range(N):
-        (okd, ovd)[i % 2][(i // 2) * part_cols:(i // 2 + 1) * part_cols, :] = res[i].astype(F32)
 
     for j in range(1, span):
         @pl.when(w + j < W)
@@ -338,6 +332,16 @@
     for o in range(1, N):
         part_copy(o).wait_send()
         res_copy(o, n).wait_send()
+
+
+def widen(res, fin, okd, ovd, oku, ovu):
+    part_cols = res.shape[1]
+    piece = fin.shape[2]
+    for i in range(fin.shape[0]):
+        oku[i * piece:(i + 1) * piece, :] = fin[i, 0].astype(F32)
+        ovu[i * piece:(i + 1) * piece, :] = fin[i, 1].astype(F32)
+    for i in range(res.shape[0]):
+        (okd, ovd)[i % 2][(i // 2) * part_cols:(i // 2 + 1) * part_cols, :] = res[i].astype(F32)
 
 
 def by_kernel(file_lengths, queries, out_grad, mem_key, memory_values, enc_rows, key_down, key_up, value_down, value_up):
@@ -350,18 +354,16 @@
     half = share // 2
     piece = rank // W
     dma = pltpu.SemaphoreType.DMA
-    any_spec = pl.BlockSpec(memory_space=pl.ANY)
+    any_spec = pl.BlockSpec(memory_space=pltpu.HBM)
     vmem_spec = pl.BlockSpec(memory_space=pltpu.VMEM)
-    return pl.pallas_call(
+    res, fin = pl.pallas_call(
         functools.partial(kernel, W, N, span),
         out_shape=(
-            jax.ShapeDtypeStruct((share, rank), F32),
-            jax.ShapeDtypeStruct((share, rank), F32),
-            jax.ShapeDtypeStruct((rank, cols), F32),
-            jax.ShapeDtypeStruct((rank, cols), F32),
+            jax.ShapeDtypeStruct((N, half, rank), BF16),
+            jax.ShapeDtypeStruct((W, 2, piece, cols), BF16),
         ),
         in_specs=[pl.BlockSpec(memory_space=pltpu.SMEM)] + [any_spec] * 9,
-        out_specs=(vmem_spec,) * 4,
+        out_specs=(vmem_spec,) * 2,
         scratch_shapes=[
             pltpu.VMEM(queries.shape, BF16),
             pltpu.VMEM(out_grad.shape, BF16),
@@ -383,8 +385,6 @@
             pltpu.VMEM((W, rows, rank), BF16),
             pltpu.VMEM((W, 2, piece, cols), BF16),
             pltpu.VMEM((W, 2, piece, cols), BF16),
-            pltpu.VMEM((W, 2, piece, cols), BF16),
-            pltpu.VMEM((N, half, rank), BF16),
             dma((10,)),
             dma((span, 2)), dma((span, 2)),
             dma((W,)), dma((W,)),
@@ -396,9 +396,20 @@
             dma((N,)), dma((N,)),
         ],
         compiler_params=pltpu.CompilerParams(
-            collective_id=0, has_side_effects=True, vmem_limit_bytes=48 * 2**20
+            collective_id=0, has_side_effects=True, vmem_limit_bytes=60 * 2**20
         ),
     )(file_lengths, queries, out_grad, mem_key, memory_values, enc_rows, key_down, key_up, value_down, value_up)
+    return pl.pallas_call(
+        widen,
+        out_shape=(
+            jax.ShapeDtypeStruct((share, rank), F32),
+            jax.ShapeDtypeStruct((share, rank), F32),
+            jax.ShapeDtypeStruct((rank, cols), F32),
+            jax.ShapeDtypeStruct((rank, cols), F32),
+        ),
+        in_specs=[vmem_spec] * 2,
+        out_specs=(vmem_spec,) * 4,
+    )(res, fin)
 
 
 def solution(mesh):

time: 66.6 us -> 56.9 us (0.85)
  local copies, waits for them, and re-layouts: 11.6 us -> 0 us
  Pallas kernels: 53.8 us -> 56 us
    unnamed x22 -> x0, local copies, waits for them, and re-layouts: 11.6 us -> none
    pallas_call x0 -> x1, Pallas kernels: none -> 1.88 us  [by_kernel(): pl.pallas_call(widen, out_shape=(jax.ShapeDtypeStruct((share, rank), F32)...]
where the time goes in v2:
time: 56.9 us; the launch traced here: 56.7 us
  Pallas kernels  56 us (98%)
  between operations  0.64 us (1%)
    pallas_call x1, Pallas kernels, by_kernel(): pl.pallas_call(functools.partial(kernel, W, N, span), out_shape=(jax.Shap...  54.2 us
    pallas_call x1, Pallas kernels, by_kernel(): pl.pallas_call(widen, out_shape=(jax.ShapeDtypeStruct((share, rank), F32)...  1.88 us

profile of v2, /device:TPU:0, one launch (start us, length us, event | category | flops | bytes accessed | tf_op | source)
XLA Modules:
  0.0 56.7 jit_solution(10882678272435399545)
XLA Ops:
  0.6 54.2 %shard_map.129 = (bf16[4,256,128]{2,1,0:T(8,128)(2,1)}, bf16[8,2,16,256]{3,2,1,0:T(8,128)(2,1)}) custom-call(s32[3]{0:T(128)} %lengths.1, bf16[512,1024]{1,0:T(8,128)(2,1)} %q_hbm.1, bf16[512,1024]{1,0:T(8,128)(2,1)} %g_hbm.1, bf16[128,256]{1,0:T(8,128)(2,1)} %k_hbm.1, bf16[128,256]{1,0:T(8,128)(2,1)} %v_hbm.1, bf16[128,4096]{1,0:T(8,128)(2,1)} %enc_hbm.1, ...), custom_call_target="tpu_custom_call" | custom-call | tf_op jit(solution)/shard_map/pallas_call | solution.py:359
  54.8 1.9 %shard_map.130 = (f32[512,128]{1,0:T(8,128)}, f32[512,128]{1,0:T(8,128)}, f32[128,256]{1,0:T(8,128)}, f32[128,256]{1,0:T(8,128)}) custom-call(bf16[4,256,128]{2,1,0:T(8,128)(2,1)} %get-tuple-element.6.res, bf16[8,2,16,256]{3,2,1,0:T(8,128)(2,1)} %get-tuple-element.7.fin), custom_call_target="tpu_custom_call" | custom-call | tf_op jit(solution)/shard_map/pallas_call | solution.py:402

commit v3 on v2

--- a/solution.py
+++ b/solution.py
@@ -171,11 +171,6 @@
     for o in range(1, W):
         enc_copy(o).start()
 
-    l_enc.wait()
-    l_kd.wait()
-    l_vd.wait()
-    u_v[...] = jnp.dot(enc_v[...], down_v[...], preferred_element_type=F32).astype(BF16)
-
     position = position_of(lengths, w)
     bias = [jnp.where(j <= position, 0.0, -1e30).astype(F32) for j in range(span)]
     l_k.wait()
@@ -188,7 +183,7 @@
             kv_copy(j, 0).wait_recv()
             kv_copy(j, 1).wait_recv()
     factor = scale * math.log2(math.e)
-    chunk = 256
+    chunk = 512
     n_chunks = q_v.shape[0] // chunk
 
     def c_copy(g, j):
@@ -228,6 +223,11 @@
             @pl.when(w >= j)
             def _():
                 c_copy(g, j).start()
+
+    l_enc.wait()
+    l_kd.wait()
+    l_vd.wait()
+    u_v[...] = jnp.dot(enc_v[...], down_v[...], preferred_element_type=F32).astype(BF16)
 
     for g in range(groups):
         for j in range(1, span):

time: 56.9 us -> 55.9 us (0.982)
  Pallas kernels: 56 us -> 55.1 us
    pallas_call x1, Pallas kernels: 54.2 us -> 53.2 us  [by_kernel(): pl.pallas_call(functools.partial(kernel, W, N, span), out_shape=(jax.Shap...]
where the time goes in v3:
time: 55.9 us; the launch traced here: 55.7 us
  Pallas kernels  55.1 us (99%)
  between operations  0.64 us (1%)
    pallas_call x1, Pallas kernels, by_kernel(): pl.pallas_call(functools.partial(kernel, W, N, span), out_shape=(jax.Shap...  53.2 us
    pallas_call x1, Pallas kernels, by_kernel(): pl.pallas_call(widen, out_shape=(jax.ShapeDtypeStruct((share, rank), F32)...  1.88 us

profile of v3, /device:TPU:0, one launch (start us, length us, event | category | flops | bytes accessed | tf_op | source)
XLA Modules:
  0.0 55.7 jit_solution(5625537344912478880)
XLA Ops:
  0.6 53.2 %shard_map.129 = (bf16[4,256,128]{2,1,0:T(8,128)(2,1)}, bf16[8,2,16,256]{3,2,1,0:T(8,128)(2,1)}) custom-call(s32[3]{0:T(128)} %lengths.1, bf16[512,1024]{1,0:T(8,128)(2,1)} %q_hbm.1, bf16[512,1024]{1,0:T(8,128)(2,1)} %g_hbm.1, bf16[128,256]{1,0:T(8,128)(2,1)} %k_hbm.1, bf16[128,256]{1,0:T(8,128)(2,1)} %v_hbm.1, bf16[128,4096]{1,0:T(8,128)(2,1)} %enc_hbm.1, ...), custom_call_target="tpu_custom_call" | custom-call | tf_op jit(solution)/shard_map/pallas_call | solution.py:359
  53.9 1.9 %shard_map.130 = (f32[512,128]{1,0:T(8,128)}, f32[512,128]{1,0:T(8,128)}, f32[128,256]{1,0:T(8,128)}, f32[128,256]{1,0:T(8,128)}) custom-call(bf16[4,256,128]{2,1,0:T(8,128)(2,1)} %get-tuple-element.6.res, bf16[8,2,16,256]{3,2,1,0:T(8,128)(2,1)} %get-tuple-element.7.fin), custom_call_target="tpu_custom_call" | custom-call | tf_op jit(solution)/shard_map/pallas_call | solution.py:402
